TPU v7x, 32 devices: a whole 2x2x4 slice. The times are simulated.
32 devices in a mesh: dp: 8 (over z, x), owner: 4 (over y, core).
Axes of the slice: x: 2, y: 2, z: 4, core: 2. Of those that a mesh axis runs over, the one named last changes fastest.
Arguments:
- hidden: bfloat16 [8192, 6912], P(('dp', 'owner')), may hold values from -6 to 6
- grad_out: bfloat16 [8192, 2560], P(('dp', 'owner')), may hold values from -6 to 6
- block_list: int32 [128, 2], replicated, may hold values from 0 to 107, as said below
- live_block_count: int32 [32], replicated, may hold values from 1 to 4, as said below
- master: float32 [128, 4096], P(('dp', 'owner')), may hold values from -6 to 6
- moment: float32 [128, 4096], P(('dp', 'owner')), may hold values from -6 to 6
- variance: float32 [128, 4096], P(('dp', 'owner')), may hold values from 0.25 to 4
Outputs:
- new_master: float32 [128, 4096], P(('dp', 'owner'))
- new_moment: float32 [128, 4096], P(('dp', 'owner'))
- new_variance: float32 [128, 4096], P(('dp', 'owner'))
- clipped_grad: float32 [128, 4096], P(('dp', 'owner'))
- published: bfloat16 [128, 4096], replicated
Inputs may be any that keep to these rules, and one draw needn't show every extreme that they name: `block_list`: each row names a block: its row index below 108, its column index below 40; all rows name different blocks. Rows 4 o to 4 o + 3 are owner o's slots; owner o is the device whose index along dp is o // 4 and whose index along the mesh axis `owner` is o mod 4. Owner o's first live_block_count[o] slots are live, the rest padding; some owner's slots are all live.
All inputs are finite; a program needn't handle non-finite values.
Results may differ from a plain program's by a relative error of at most 0.001.
Values may be sent and summed in bfloat16 or wider, within the bound.
No kernel may reach another device: no remote copies, remote signals or barrier semaphores. Data moves between devices by JAX's collectives and lax.ppermute only.
A program may use at most 128 MiB of HBM per device.

v0:
```python
import math

import jax
import jax.numpy as jnp
from jax import lax
from jax.sharding import PartitionSpec as P

BLOCK_SIDE_SIZE = 64
OWNER_SLOTS = 4


def block_terms(hidden, grad_out, row_indices, column_indices, active_slot_mask, row_count):
    tok_rows = hidden.shape[0]
    block_side = BLOCK_SIDE_SIZE
    group_size = math.gcd(row_count, 8 * OWNER_SLOTS)
    hidden_blocks = hidden.reshape(tok_rows, hidden.shape[1] // block_side, block_side)
    output_blocks = grad_out.reshape(tok_rows, grad_out.shape[1] // block_side, block_side)

    def one_group(id_pair):
        row_sel, col_sel = id_pair
        left_cols = jnp.take(hidden_blocks, row_sel, axis=1)
        right_cols = jnp.take(output_blocks, col_sel, axis=1)
        products = lax.dot_general(
            left_cols, right_cols, (((0,), (0,)), ((1,), (1,))), preferred_element_type=jnp.float32
        )
        return products.reshape(group_size, block_side * block_side)

    group_terms = lax.map(
        one_group, (row_indices.reshape(-1, group_size), column_indices.reshape(-1, group_size))
    )
    group_terms = group_terms.reshape(row_count, block_side * block_side)
    return jnp.where(active_slot_mask[:, None], group_terms, jnp.zeros_like(group_terms))


def local(hidden, grad_out, block_list, live_block_count, master, moment, variance):
    slot_rows = master.shape[0]
    row_indices = block_list[:, 0]
    column_indices = block_list[:, 1]
    active_slot_mask = (
        jnp.arange(slot_rows, dtype=jnp.int32)[None, :] < live_block_count[:, None]
    ).reshape(-1)
    weight_gradient = lax.psum_scatter(
        block_terms(
            hidden,
            grad_out,
            row_indices,
            column_indices,
            active_slot_mask,
            lax.axis_size(("dp", "owner")) * slot_rows,
        ),
        ("dp", "owner"),
        scatter_dimension=0,
        tiled=True,
    )
    square_total = lax.psum(jnp.sum(weight_gradient * weight_gradient), ("dp", "owner"))
    live_total = jnp.sum(live_block_count).astype(jnp.float32) * weight_gradient.shape[1]
    mean_square = square_total / live_total
    clip_scale = jnp.minimum(1.0, 1.0 / jnp.sqrt(mean_square + 1e-06))
    clipped_grad = clip_scale * weight_gradient
    new_moment = 0.9 * moment + 0.1 * clipped_grad
    new_variance = 0.95 * variance + 0.05 * clipped_grad * clipped_grad
    moment_hat = new_moment / (1.0 - 0.9**20)
    variance_hat = new_variance / (1.0 - 0.95**20)
    new_master = master - 0.02 * (moment_hat / (jnp.sqrt(variance_hat) + 1e-08) + 0.1 * master)
    own_blocks = new_master.astype(jnp.bfloat16)
    published = lax.all_gather(own_blocks, ("dp", "owner"), axis=0, tiled=True)
    return (new_master, new_moment, new_variance, clipped_grad, published)


def solution(mesh):
    return jax.shard_map(
        local,
        mesh=mesh,
        in_specs=(
            P(("dp", "owner"), None),
            P(("dp", "owner"), None),
            P(),
            P(),
            P(("dp", "owner"), None),
            P(("dp", "owner"), None),
            P(("dp", "owner"), None),
        ),
        out_specs=(
            P(("dp", "owner"), None),
            P(("dp", "owner"), None),
            P(("dp", "owner"), None),
            P(("dp", "owner"), None),
            P(),
        ),
        check_vma=False,
    )
```

profile of v0, /device:TPU:0, one launch (start us, length us, event | category | flops | bytes accessed | tf_op | source)
XLA Modules:
  0.0 290.0 jit_solution(11210928516595766826)
XLA Ops:
  7.2 0.8 slice_reduce_fusion
  8.2 6.1 %copy.16 = bf16[256,6912]{0,1:T(8,128)(2,1)} copy(bf16[256,6912]{1,0:T(8,128)(2,1)} %param.9) | data formatting | bytes 7077888 | tf_op args[0]
  14.3 0.6 copy.17
  14.9 28.8 %while.10 = (s32[]{:T(128)}, f32[4,32,4096]{2,1,0:T(8,128)}, s32[4,32]{1,0:T(4,128)S(1)}, bf16[256,108,64]{0,2,1:T(8,128)(2,1)}, s32[4,32]{1,0:T(4,128)S(1)}, /*index=5*/bf16[256,40,64]{0,2,1:T(8,128)(2,1)S(1)}, s32[]{:T(128)}) while((s32[]{:T(128)}, f32[4,32,4096]{2,1,0:T(8,128)}, s32[4,32]{1,0:T(4,128)S(1)}, ...), condition=%wide.region_1.2_spmd, body=%wide.region_0.1_spmd.sunk | while | flops 68160064 | bytes 8923093 | solution.py:28
  14.9 0.6 gather_fusion
  15.6 2.6 gather_fusion.1
  18.2 1.5 fusion.20
  19.7 1.6 broadcast_in_dim.44
  21.3 0.8 constant_dynamic-update-slice_fusion.2
  22.1 0.6 gather_fusion
  22.7 2.6 gather_fusion.1
  25.4 1.5 fusion.20
  26.9 1.6 broadcast_in_dim.44
  28.4 0.8 constant_dynamic-update-slice_fusion.2
  29.3 0.6 gather_fusion
  29.9 2.6 gather_fusion.1
  32.6 1.5 fusion.20
  34.0 1.6 broadcast_in_dim.44
  35.6 0.8 constant_dynamic-update-slice_fusion.2
  36.5 0.6 gather_fusion
  37.1 2.6 gather_fusion.1
  39.8 1.5 fusion.20
  41.2 1.6 broadcast_in_dim.44
  42.8 0.8 constant_dynamic-update-slice_fusion.2
  43.8 3.2 %bitcast_select_fusion = f32[128,4096]{1,0:T(8,128)} fusion(f32[4,32,4096]{2,1,0:T(8,128)} %get-tuple-element.37, pred[128]{0:T(512)(128)(4,1)S(1)} %lt.64), kind=kLoop, calls=%fused_computation.24 | loop fusion | flops 524288 | bytes 4194432 | tf_op jit(solution)/shard_map/jit(_where)/select_n | solution.py:32
  47.1 0.6 reduce_sum.19
  48.4 135.3 %all-reduce.3.cloned.1.call-done = f32[128,4096]{1,0:T(8,128)} async-done(((f32[128,4096]{1,0:T(8,128)}), f32[128,4096]{1,0:T(8,128)}) %all-reduce.3.cloned.1.call-update) | async-done | bytes 2097168
  183.8 1.5 multiply_reduce_fusion
  185.3 39.3 %psum.7 = f32[]{:T(128)} all-reduce(f32[]{:T(128)} %multiply_reduce_fusion), channel_id=1, replica_groups=mesh['dp'=8,'owner'=4] {'dp','owner'}, use_global_device_ids=true, to_apply=%region_4.5 | all-reduce | flops 1 | bytes 8 | tf_op jit(solution)/shard_map/psum | solution.py:55
  225.3 1.7 convert_bitcast_fusion
  227.1 53.9 %all-gather.3.cloned.1.call-done = bf16[32,4,4096]{2,1,0:T(4,128)(2,1)} async-done(((bf16[1,4,4096]{2,1,0:T(4,128)(2,1)}), bf16[32,4,4096]{2,1,0:T(4,128)(2,1)}) %all-gather.3.cloned.1.call-update) | async-done | bytes 1048592 | tf_op jit(solution)/shard_map/all_gather | solution.py:66
  281.0 2.1 reshape.124
  (35 shorter events, 0.6 us)
Async XLA Ops:
  7.2 176.6 %all-reduce.3.cloned.1.call-start = ((), (), s32[]{:S(2)}) async-start(), calls=%async_computation.1 | async-start | bytes 4194304
  8.2 6.1 %copy-start = (bf16[256,2560]{1,0:T(8,128)(2,1)S(1)}, bf16[256,2560]{1,0:T(8,128)(2,1)}, u32[]{:S(2)}) copy-start(bf16[256,2560]{1,0:T(8,128)(2,1)} %param.10) | copy-start | bytes 3932164
  14.9 28.8 %copy-start.4 = (s32[32]{0:T(128)S(1)}, s32[32]{0:T(128)}, u32[]{:S(2)}) copy-start(s32[32]{0:T(128)} %param.12) | copy-start | bytes 388
  47.1 178.3 %copy-start.1 = (f32[4,4096]{1,0:T(4,128)S(1)}, f32[4,4096]{1,0:T(4,128)}, u32[]{:S(2)}) copy-start(f32[4,4096]{1,0:T(4,128)} %param.13) | copy-start | bytes 196612
  47.1 178.3 %copy-start.2 = (f32[4,4096]{1,0:T(4,128)S(1)}, f32[4,4096]{1,0:T(4,128)}, u32[]{:S(2)}) copy-start(f32[4,4096]{1,0:T(4,128)} %param.14) | copy-start | bytes 196612
  47.1 178.3 %copy-start.3 = (f32[4,4096]{1,0:T(4,128)S(1)}, f32[4,4096]{1,0:T(4,128)}, u32[]{:S(2)}) copy-start(f32[4,4096]{1,0:T(4,128)} %param.15) | copy-start | bytes 196612
  47.1 233.9 %all-gather.3.cloned.1.call-start = ((), (), s32[]{:S(2)}) async-start(), calls=%async_computation | async-start | bytes 1081344 | tf_op jit(solution)/shard_map/all_gather | solution.py:66
Sparse Core Ops, SparseCore 0:
  47.2 136.5 all-reduce.2
  227.2 53.7 all-gather.2
where the time goes:
time: 291 us; the launch traced here: 290 us
  waiting for transfers between devices  189 us (65%)
  blocking collectives  39.3 us (14%)
  local copies, waits for them, and re-layouts  32.4 us (11%)
  between operations  15.5 us (5%)
  other arithmetic  7.3 us (3%)
  matrix products  5.92 us (2%)
    unnamed x3, waiting for transfers between devices  135 us
    all_gather x1, waiting for transfers between devices, local(): published = lax.all_gather(own_blocks, ('dp', 'owner'), axis=0, tiled=True)  53.9 us
    psum x1, blocking collectives, local(): lax.psum(jnp.sum(weight_gradient * weight_gradient), ('dp', 'owner'))  39.3 us
    gather x4, local copies, waits for them, and re-layouts, one_group(): left_cols = jnp.take(hidden_blocks, row_sel, axis=1)  10.5 us
    unnamed x13, local copies, waits for them, and re-layouts  8.84 us
    broadcast_in_dim x4, local copies, waits for them, and re-layouts, block_terms(): lax.map(one_group, (row_indices.reshape(-1, group_size), column_indices.r...  6.32 us
    dot_general x4, matrix products, one_group(): lax.dot_general(left_cols, right_cols, (((0,), (0,)), ((1,), (1,))), pref...  5.92 us
  transfers between devices with their start and end apart: 2, of which 2 were waited for; matrix products, arithmetic and copies ran while one was open for 0% of the time, Pallas kernels for 0%

commit v1 on v0

v1 whole, which is shorter than its diff:
```python
import functools

import jax
import jax.numpy as jnp
from jax import lax
from jax.experimental import pallas as pl
from jax.experimental.pallas import tpu as pltpu
from jax.sharding import PartitionSpec as P

SIDE = 64
LANES = 128
SLOTS = 4
BLOCK = SIDE * SIDE
TILES = BLOCK // LANES
HALF = TILES // 2
CODE_ROWS = HALF * SLOTS
EXP_ROWS = 8
CODE_BITS = 13
AXES = ("dp", "owner")
INV_LN2 = 1.4426950408889634


def terms_kernel(blocks_ref, hidden_ref, grad_ref, out_ref, prod_ref):
    owners = out_ref.shape[0]
    low_lane = lax.broadcasted_iota(jnp.int32, (TILES, LANES), 1) < SIDE

    def one_owner(o, carry):
        packed = []
        for s in range(SLOTS):
            r = blocks_ref[0, o * SLOTS + s]
            c = blocks_ref[1, o * SLOTS + s]
            left = hidden_ref[:, pl.ds(pl.multiple_of((r // 2) * LANES, LANES), LANES)]
            right = grad_ref[:, pl.ds(pl.multiple_of((c // 2) * LANES, LANES), LANES)]
            prod_ref[s] = lax.dot_general(
                left, right, (((0,), (0,)), ((), ())), preferred_element_type=jnp.float32
            )
            base = (r % 2) * SIDE
            even = prod_ref[s, pl.ds(base, TILES, stride=2), :]
            odd = prod_ref[s, pl.ds(base + 1, TILES, stride=2), :]
            crossed = pltpu.roll(jnp.where(low_lane, odd, even), SIDE, 1)
            first_half = c % 2 == 0
            keep_even = jnp.where(first_half, even, crossed)
            keep_odd = jnp.where(first_half, crossed, odd)
            packed.append(jnp.where(low_lane, keep_even, keep_odd))
        peak = functools.reduce(jnp.maximum, [jnp.abs(p) for p in packed])
        peak = jnp.max(peak, axis=0, keepdims=True)
        exponent = jnp.floor(jnp.log(jnp.maximum(peak, 1e-30)) * INV_LN2)
        scale = jnp.exp2(CODE_BITS - exponent)
        for s in range(SLOTS):
            code = jnp.round(packed[s] * scale).astype(jnp.int32)
            word = (code[:HALF] << 16) | (code[HALF:] & 0xFFFF)
            out_ref[o, pl.ds(s, HALF, stride=SLOTS), :] = word
        out_ref[o, pl.ds(CODE_ROWS, EXP_ROWS), :] = jnp.broadcast_to(
            exponent.astype(jnp.int32), (EXP_ROWS, LANES)
        )
        return carry

    lax.fori_loop(0, owners, one_owner, 0)


def sum_kernel(live_ref, recv_ref, grad_ref, square_ref):
    owners = recv_ref.shape[0]

    def add(d, totals):
        high, low = totals
        word = recv_ref[d, pl.ds(0, CODE_ROWS), :]
        exponent = recv_ref[d, pl.ds(CODE_ROWS, EXP_ROWS), :][:1].astype(jnp.float32)
        scale = jnp.exp2(exponent - CODE_BITS)
        high = high + (word >> 16).astype(jnp.float32) * scale
        low = low + ((word << 16) >> 16).astype(jnp.float32) * scale
        return high, low

    zero = jnp.zeros((CODE_ROWS, LANES), jnp.float32)
    high, low = lax.fori_loop(0, owners, add, (zero, zero), unroll=4)
    slot = lax.broadcasted_iota(jnp.int32, (CODE_ROWS, LANES), 0) % SLOTS
    live = slot < live_ref[0]
    high = jnp.where(live, high, 0.0)
    low = jnp.where(live, low, 0.0)
    grad_ref[pl.ds(0, CODE_ROWS), :] = high
    grad_ref[pl.ds(CODE_ROWS, CODE_ROWS), :] = low
    square_ref[...] = jnp.broadcast_to(
        jnp.sum(high * high + low * low, keepdims=True), square_ref.shape
    )


def update_kernel(
    live_total_ref, square_ref, grad_ref, master_ref, moment_ref, variance_ref,
    new_master_ref, new_moment_ref, new_variance_ref, clipped_ref, own_ref,
):
    entries = jnp.full((1, LANES), live_total_ref[0], jnp.int32).astype(jnp.float32) * BLOCK
    mean_square = square_ref[:1] / entries
    clip = jnp.minimum(1.0, 1.0 / jnp.sqrt(mean_square + 1e-06))
    for t in range(TILES):
        lanes = pl.ds(t * LANES, LANES)
        clipped = clip * grad_ref[pl.ds(t * SLOTS, SLOTS), :]
        moment = 0.9 * moment_ref[:, lanes] + 0.1 * clipped
        variance = 0.95 * variance_ref[:, lanes] + 0.05 * clipped * clipped
        master = master_ref[:, lanes]
        moment_hat = moment / (1.0 - 0.9**20)
        variance_hat = variance / (1.0 - 0.95**20)
        step = moment_hat / (jnp.sqrt(variance_hat) + 1e-08) + 0.1 * master
        master = master - 0.02 * step
        clipped_ref[:, lanes] = clipped
        new_moment_ref[:, lanes] = moment
        new_variance_ref[:, lanes] = variance
        new_master_ref[:, lanes] = master
        own_ref[:, lanes] = master.astype(jnp.bfloat16)


VMEM = pl.BlockSpec(memory_space=pltpu.VMEM)
SMEM = pl.BlockSpec(memory_space=pltpu.SMEM)
PARAMS = pltpu.CompilerParams(vmem_limit_bytes=40 * 1024 * 1024)


def local(hidden, grad_out, block_list, live_block_count, master, moment, variance):
    owners = lax.axis_size(AXES)
    tokens = hidden.shape[0]
    me = lax.axis_index(AXES)
    codes = pl.pallas_call(
        terms_kernel,
        out_shape=jax.ShapeDtypeStruct((owners, CODE_ROWS + EXP_ROWS, LANES), jnp.int32),
        in_specs=[SMEM, VMEM, VMEM],
        out_specs=VMEM,
        scratch_shapes=[pltpu.VMEM((SLOTS, LANES, LANES), jnp.float32)],
        compiler_params=PARAMS,
        cost_estimate=pl.CostEstimate(
            flops=2 * owners * SLOTS * LANES * LANES * tokens,
            bytes_accessed=2 * (hidden.size + grad_out.size),
            transcendentals=0,
        ),
        name="block_terms",
    )(block_list.T, hidden, grad_out)
    received = lax.all_to_all(codes, AXES, split_axis=0, concat_axis=0, tiled=True)
    gradient, square = pl.pallas_call(
        sum_kernel,
        out_shape=(
            jax.ShapeDtypeStruct((TILES * SLOTS, LANES), jnp.float32),
            jax.ShapeDtypeStruct((8, LANES), jnp.float32),
        ),
        in_specs=[SMEM, VMEM],
        out_specs=(VMEM, VMEM),
        compiler_params=PARAMS,
        name="sum_sources",
    )(lax.dynamic_slice(live_block_count, (me,), (1,)), received)
    distance = 1
    while distance < owners:
        pairs = [(i, i ^ distance) for i in range(owners)]
        square = square + lax.ppermute(square, AXES, pairs)
        distance *= 2
    shape = jax.ShapeDtypeStruct(master.shape, jnp.float32)
    new_master, new_moment, new_variance, clipped, own = pl.pallas_call(
        update_kernel,
        out_shape=(shape, shape, shape, shape, jax.ShapeDtypeStruct(master.shape, jnp.bfloat16)),
        in_specs=[SMEM, VMEM, VMEM, VMEM, VMEM, VMEM],
        out_specs=(VMEM,) * 5,
        compiler_params=PARAMS,
        name="adamw",
    )(jnp.sum(live_block_count).reshape(1), square, gradient, master, moment, variance)
    spread = jnp.broadcast_to(own[None], (owners,) + own.shape)
    published = lax.all_to_all(spread, AXES, split_axis=0, concat_axis=0, tiled=True)
    return new_master, new_moment, new_variance, clipped, published.reshape(-1, BLOCK)


def solution(mesh):
    rows = P(AXES, None)
    return jax.shard_map(
        local,
        mesh=mesh,
        in_specs=(rows, rows, P(), P(), rows, rows, rows),
        out_specs=(rows, rows, rows, rows, P()),
        check_vma=False,
    )
```

time: 291 us -> 106 us (0.36)
  waiting for transfers between devices: 189 us -> 39.9 us
  local copies, waits for them, and re-layouts: 32.4 us -> 6.14 us
  Pallas kernels: 0 us -> 16.7 us
  between operations: 15.5 us -> 0.71 us
  starting transfers between devices: 0.08 us -> 11.8 us
  blocking collectives: 39.3 us -> 29.6 us
  other arithmetic: 7.3 us -> 0.65 us
  matrix products: 5.92 us -> 0 us
    unnamed x3 -> x0, waiting for transfers between devices: 135 us -> none
    all_gather x1 -> x0, waiting for transfers between devices: 53.9 us -> none  [local(): published = lax.all_gather(own_blocks, ('dp', 'owner'), axis=0, tiled=True)]
    psum x1 -> x0, blocking collectives: 39.3 us -> none  [local(): lax.psum(jnp.sum(weight_gradient * weight_gradient), ('dp', 'owner'))]
    all_to_all x0 -> x1, blocking collectives: none -> 29.6 us  [local(): lax.all_to_all(spread, AXES, split_axis=0, concat_axis=0, tiled=True)]
    all_to_all x0 -> x1, waiting for transfers between devices: none -> 28.5 us  [local(): lax.all_to_all(codes, AXES, split_axis=0, concat_axis=0, tiled=True)]
    pallas_call x0 -> x3, Pallas kernels: none -> 16.7 us  [the longest x1 14.1 us: local(): pl.pallas_call(terms_kernel, out_shape=jax.ShapeDtypeStruct((owners, CODE...]
    gather x8 -> x0, local copies, waits for them, and re-layouts: 12.9 us -> none  [the longest x4 10.5 us: one_group(): left_cols = jnp.take(hidden_blocks, row_sel, axis=1)]
    ppermute x0 -> x5, waiting for transfers between devices: none -> 11.4 us  [local(): square = square + lax.ppermute(square, AXES, pairs)]
  transfers between devices with their start and end apart: 2 -> 6, of which waited for: 2 -> 6; matrix products, arithmetic and copies ran while one was open for 0% -> 1% of each run, Pallas kernels for 0% -> 0%
where the time goes in v1:
time: 106 us
  waiting for transfers between devices  39.9 us (38%)
  blocking collectives  29.6 us (28%)
  Pallas kernels  16.7 us (16%)
  starting transfers between devices  11.8 us (11%)
  local copies, waits for them, and re-layouts  6.14 us (6%)
    all_to_all x1, blocking collectives, local(): lax.all_to_all(spread, AXES, split_axis=0, concat_axis=0, tiled=True)  29.6 us
    all_to_all x1, waiting for transfers between devices, local(): lax.all_to_all(codes, AXES, split_axis=0, concat_axis=0, tiled=True)  28.5 us
    pallas_call x1, Pallas kernels, local(): pl.pallas_call(terms_kernel, out_shape=jax.ShapeDtypeStruct((owners, CODE...  14.1 us
    ppermute x5, waiting for transfers between devices, local(): square = square + lax.ppermute(square, AXES, pairs)  11.4 us
    all_to_all x1, starting transfers between devices, local(): lax.all_to_all(codes, AXES, split_axis=0, concat_axis=0, tiled=True)  7.3 us
    ppermute x5, starting transfers between devices, local(): square = square + lax.ppermute(square, AXES, pairs)  4.51 us
    unnamed x14, local copies, waits for them, and re-layouts  4 us
  transfers between devices with their start and end apart: 6, of which 6 were waited for; matrix products, arithmetic and copies ran while one was open for 1% of the time, Pallas kernels for 0%

profile of v1, /device:TPU:0, one launch (start us, length us, event | category | flops | bytes accessed | tf_op | source)
XLA Modules:
  0.0 105.6 jit_solution(3231514940442544043)
XLA Ops:
  0.6 0.0 copy-start
  0.6 2.0 %copy-done = bf16[256,6912]{1,0:T(8,128)(2,1)S(1)} copy-done((bf16[256,6912]{1,0:T(8,128)(2,1)S(1)}, bf16[256,6912]{1,0:T(8,128)(2,1)}, u32[]{:S(2)}) %copy-start) | copy-done | bytes 3538968
  2.6 0.0 copy-start.1
  2.6 1.3 %copy-done.1 = bf16[256,2560]{1,0:T(8,128)(2,1)S(1)} copy-done((bf16[256,2560]{1,0:T(8,128)(2,1)S(1)}, bf16[256,2560]{1,0:T(8,128)(2,1)}, u32[]{:S(2)}) %copy-start.1) | copy-done | bytes 1310744
  4.0 0.0 copy-start.5
  4.0 0.7 copy-done.5
  4.6 14.1 %block_terms.1 = s32[32,72,128]{2,1,0:T(8,128)} custom-call(s32[2,128]{1,0:T(2,128)S(1)} %bitcast.2, bf16[256,6912]{1,0:T(8,128)(2,1)S(1)} %copy-done, bf16[256,2560]{1,0:T(8,128)(2,1)S(1)} %copy-done.1), custom_call_target="tpu_custom_call" | custom-call | flops 1073741824 | bytes 4849664 | tf_op jit(solution)/shard_map/block_terms/pallas_call | solution.py:119
  18.8 0.0 copy-start.6
  18.8 0.0 copy-start.2
  18.8 7.3 %all-to-all-start = ((s32[32,72,128]{2,1,0:T(8,128)}), s32[32,72,128]{2,1,0:T(8,128)S(1)}, u32[]{:S(2)}, u32[]{:S(2)}) async-start(s32[32,72,128]{2,1,0:T(8,128)} %block_terms.1), calls=%async_computation | async-start | bytes 2359296 | tf_op jit(solution)/shard_map/all_to_all | solution.py:133
  26.1 0.0 copy-done.6
  26.1 0.6 dynamic_slice.3.live_ref
  26.7 28.5 %all-to-all-done.recv_ref = s32[32,72,128]{2,1,0:T(8,128)S(1)} async-done(((s32[32,72,128]{2,1,0:T(8,128)}), s32[32,72,128]{2,1,0:T(8,128)S(1)}, u32[]{:S(2)}, u32[]{:S(2)}) %all-to-all-start) | async-done | bytes 1179680 | tf_op jit(solution)/shard_map/all_to_all | solution.py:133
  55.2 1.2 %sum_sources.1 = (f32[128,128]{1,0:T(8,128)S(1)}, f32[8,128]{1,0:T(8,128)S(1)}) custom-call(s32[1]{0:T(128)} %dynamic_slice.3.live_ref, s32[32,72,128]{2,1,0:T(8,128)S(1)} %all-to-all-done.recv_ref), custom_call_target="tpu_custom_call" | custom-call | tf_op jit(solution)/shard_map/sum_sources/pallas_call | solution.py:134
  56.3 0.1 collective-permute-start
  56.4 1.2 %collective-permute-done = f32[8,128]{1,0:T(8,128)S(1)} collective-permute-done((f32[8,128]{1,0:T(8,128)S(1)}, f32[8,128]{1,0:T(8,128)S(1)}, u32[]{:S(2)}, u32[]{:S(2)}) %collective-permute-start) | collective-permute-done | bytes 4128 | tf_op jit(solution)/shard_map/ppermute | solution.py:148
  57.6 1.4 %collective-permute-start.1 = (f32[8,128]{1,0:T(8,128)S(1)}, f32[8,128]{1,0:T(8,128)S(1)}, u32[]{:S(2)}, u32[]{:S(2)}) collective-permute-start(f32[8,128]{1,0:T(8,128)S(1)} %add.23), channel_id=1, source_target_pairs={{0,2},{1,3},{2,0},{3,1},{4,6},{5,7},{6,4},{7,5},{8,10},{9,11},{10,... | collective-permute-start | bytes 12296 | tf_op jit(solution)/shard_map/ppermute | solution.py:148
  59.0 2.2 %collective-permute-done.1 = f32[8,128]{1,0:T(8,128)S(1)} collective-permute-done((f32[8,128]{1,0:T(8,128)S(1)}, f32[8,128]{1,0:T(8,128)S(1)}, u32[]{:S(2)}, u32[]{:S(2)}) %collective-permute-start.1) | collective-permute-done | bytes 4128 | tf_op jit(solution)/shard_map/ppermute | solution.py:148
  61.2 1.4 %collective-permute-start.2 = (f32[8,128]{1,0:T(8,128)S(1)}, f32[8,128]{1,0:T(8,128)S(1)}, u32[]{:S(2)}, u32[]{:S(2)}) collective-permute-start(f32[8,128]{1,0:T(8,128)S(1)} %add.24), channel_id=1, source_target_pairs={{0,4},{1,5},{2,6},{3,7},{4,0},{5,1},{6,2},{7,3},{8,12},{9,13},{10,... | collective-permute-start | bytes 12296 | tf_op jit(solution)/shard_map/ppermute | solution.py:148
  62.6 2.2 %collective-permute-done.2 = f32[8,128]{1,0:T(8,128)S(1)} collective-permute-done((f32[8,128]{1,0:T(8,128)S(1)}, f32[8,128]{1,0:T(8,128)S(1)}, u32[]{:S(2)}, u32[]{:S(2)}) %collective-permute-start.2) | collective-permute-done | bytes 4128 | tf_op jit(solution)/shard_map/ppermute | solution.py:148
  64.8 0.5 collective-permute-start.3
  65.3 3.1 %collective-permute-done.3 = f32[8,128]{1,0:T(8,128)S(1)} collective-permute-done((f32[8,128]{1,0:T(8,128)S(1)}, f32[8,128]{1,0:T(8,128)S(1)}, u32[]{:S(2)}, u32[]{:S(2)}) %collective-permute-start.3) | collective-permute-done | bytes 4128 | tf_op jit(solution)/shard_map/ppermute | solution.py:148
  68.4 1.1 collective-permute-start.4
  69.5 0.6 reduce_sum.9
  70.1 2.8 %collective-permute-done.4 = f32[8,128]{1,0:T(8,128)S(1)} collective-permute-done((f32[8,128]{1,0:T(8,128)S(1)}, f32[8,128]{1,0:T(8,128)S(1)}, u32[]{:S(2)}, u32[]{:S(2)}) %collective-permute-start.4) | collective-permute-done | bytes 4128 | tf_op jit(solution)/shard_map/ppermute | solution.py:148
  72.9 0.0 copy-done.2
  72.9 0.0 copy-done.3
  72.9 0.0 copy-done.4
  72.9 1.4 %adamw.1 = (f32[4,4096]{1,0:T(4,128)}, f32[4,4096]{1,0:T(4,128)}, f32[4,4096]{1,0:T(4,128)}, f32[4,4096]{1,0:T(4,128)}, bf16[4,4096]{1,0:T(4,128)(2,1)S(1)}) custom-call(s32[1]{0:T(128)} %bitcast.live_total_ref, f32[8,128]{1,0:T(8,128)S(1)} %add.27.square_ref, f32[128,128]{1,0:T(8,128)S(1)} %get-tuple-element.13.grad_ref, f32[4,4096]{1,0:T(4,128)S(1)} %copy-done.2, ...), custom_call_target="tpu_custom_call" | custom-call | tf_op jit(solution)/shard_map/adamw/pallas_call | solution.py:151
  74.4 0.5 broadcast_in_dim.2
  74.9 29.6 %all_to_all.10 = bf16[32,4,4096]{2,1,0:T(4,128)(2,1)S(1)} all-to-all(bf16[32,4,4096]{2,1,0:T(4,128)(2,1)S(1)} %broadcast_in_dim.2), channel_id=1, replica_groups=mesh['dp'=8,'owner'=4] {'dp','owner'}, dimensions={0} | all-to-all | bytes 2097152 | tf_op jit(solution)/shard_map/all_to_all | solution.py:160
  104.5 1.1 %reshape.18 = bf16[128,4096]{1,0:T(8,128)(2,1)} reshape(bf16[32,4,4096]{2,1,0:T(4,128)(2,1)S(1)} %all_to_all.10) | data formatting | bytes 2097152 | tf_op jit(solution)/shard_map/reshape | solution.py:161
  (7 shorter events, 0.0 us)
Async XLA Ops:
  0.6 2.0 %copy-start = (bf16[256,6912]{1,0:T(8,128)(2,1)S(1)}, bf16[256,6912]{1,0:T(8,128)(2,1)}, u32[]{:S(2)}) copy-start(bf16[256,6912]{1,0:T(8,128)(2,1)} %hidden_ref.1) | copy-start | bytes 10616836
  2.6 1.3 %copy-start.1 = (bf16[256,2560]{1,0:T(8,128)(2,1)S(1)}, bf16[256,2560]{1,0:T(8,128)(2,1)}, u32[]{:S(2)}) copy-start(bf16[256,2560]{1,0:T(8,128)(2,1)} %grad_ref.1) | copy-start | bytes 3932164
  4.0 0.7 copy-start.5
  18.8 7.3 %copy-start.6 = (s32[32]{0:T(128)S(1)}, s32[32]{0:T(128)}, u32[]{:S(2)}) copy-start(s32[32]{0:T(128)} %param.10) | copy-start | bytes 388
  18.8 54.2 %copy-start.2 = (f32[4,4096]{1,0:T(4,128)S(1)}, f32[4,4096]{1,0:T(4,128)}, u32[]{:S(2)}) copy-start(f32[4,4096]{1,0:T(4,128)} %master_ref.1) | copy-start | bytes 196612
  18.8 54.2 %copy-start.3 = (f32[4,4096]{1,0:T(4,128)S(1)}, f32[4,4096]{1,0:T(4,128)}, u32[]{:S(2)}) copy-start(f32[4,4096]{1,0:T(4,128)} %moment_ref.1) | copy-start | bytes 196612
  18.8 54.2 %copy-start.4 = (f32[4,4096]{1,0:T(4,128)S(1)}, f32[4,4096]{1,0:T(4,128)}, u32[]{:S(2)}) copy-start(f32[4,4096]{1,0:T(4,128)} %variance_ref.1) | copy-start | bytes 196612
  18.8 36.4 %all-to-all-start = ((s32[32,72,128]{2,1,0:T(8,128)}), s32[32,72,128]{2,1,0:T(8,128)S(1)}, u32[]{:S(2)}, u32[]{:S(2)}) async-start(s32[32,72,128]{2,1,0:T(8,128)} %block_terms.1), calls=%async_computation | async-start | bytes 2359296 | tf_op jit(solution)/shard_map/all_to_all | solution.py:133
  56.3 1.2 %collective-permute-start = (f32[8,128]{1,0:T(8,128)S(1)}, f32[8,128]{1,0:T(8,128)S(1)}, u32[]{:S(2)}, u32[]{:S(2)}) collective-permute-start(f32[8,128]{1,0:T(8,128)S(1)} %get-tuple-element.12), channel_id=1, source_target_pairs={{0,1},{1,0},{2,3},{3,2},{4,5},{5,4},{6,7},{7,6},{8,9},{9,8},{10,11... | collective-permute-start | bytes 12296 | tf_op jit(solution)/shard_map/ppermute | solution.py:148
  57.6 3.6 %collective-permute-start.1 = (f32[8,128]{1,0:T(8,128)S(1)}, f32[8,128]{1,0:T(8,128)S(1)}, u32[]{:S(2)}, u32[]{:S(2)}) collective-permute-start(f32[8,128]{1,0:T(8,128)S(1)} %add.23), channel_id=1, source_target_pairs={{0,2},{1,3},{2,0},{3,1},{4,6},{5,7},{6,4},{7,5},{8,10},{9,11},{10,... | collective-permute-start | bytes 12296 | tf_op jit(solution)/shard_map/ppermute | solution.py:148
  61.2 3.6 %collective-permute-start.2 = (f32[8,128]{1,0:T(8,128)S(1)}, f32[8,128]{1,0:T(8,128)S(1)}, u32[]{:S(2)}, u32[]{:S(2)}) collective-permute-start(f32[8,128]{1,0:T(8,128)S(1)} %add.24), channel_id=1, source_target_pairs={{0,4},{1,5},{2,6},{3,7},{4,0},{5,1},{6,2},{7,3},{8,12},{9,13},{10,... | collective-permute-start | bytes 12296 | tf_op jit(solution)/shard_map/ppermute | solution.py:148
  64.8 3.6 %collective-permute-start.3 = (f32[8,128]{1,0:T(8,128)S(1)}, f32[8,128]{1,0:T(8,128)S(1)}, u32[]{:S(2)}, u32[]{:S(2)}) collective-permute-start(f32[8,128]{1,0:T(8,128)S(1)} %add.25), channel_id=1, source_target_pairs={{0,8},{1,9},{2,10},{3,11},{4,12},{5,13},{6,14},{7,15},{8,0},{9,1},... | collective-permute-start | bytes 12296 | tf_op jit(solution)/shard_map/ppermute | solution.py:148
  68.4 4.5 %collective-permute-start.4 = (f32[8,128]{1,0:T(8,128)S(1)}, f32[8,128]{1,0:T(8,128)S(1)}, u32[]{:S(2)}, u32[]{:S(2)}) collective-permute-start(f32[8,128]{1,0:T(8,128)S(1)} %add.26), channel_id=1, source_target_pairs={{0,16},{1,17},{2,18},{3,19},{4,20},{5,21},{6,22},{7,23},{8,24},{9,... | collective-permute-start | bytes 12296 | tf_op jit(solution)/shard_map/ppermute | solution.py:148
